TPU v7x, 32 devices: a whole 2x2x4 slice. The times are simulated.
32 devices in a mesh: groups: 2 (over y), ep: 8 (over z, core), rep: 2 (over x).
Axes of the slice: x: 2, y: 2, z: 4, core: 2. Of those that a mesh axis runs over, the one named last changes fastest.
Arguments:
- tokens: bfloat16 [1024, 2048], P(('groups', 'ep')), parts along dimension 0, may hold values from -6 to 6
- choices: int32 [1024, 8], P(('groups', 'ep')), parts along dimension 0, may hold values from 0 to 15, all different within a row; in each aligned block of 64 rows (0 to 63, 64 to 127, ...) at most 64 rows name the same one
- route_weight: float32 [1024, 8], P(('groups', 'ep')), parts along dimension 0, may hold values from 0.05 to 0.3
- gate_proj: bfloat16 [16, 2048, 768], P('ep', None, 'rep'), may hold values from -0.125 to 0.125
- up_proj: bfloat16 [16, 2048, 768], P('ep', None, 'rep'), may hold values from -0.125 to 0.125
- down_proj: bfloat16 [16, 768, 2048], P('ep', 'rep'), may hold values from -0.21875 to 0.21875
Outputs:
- mixed: bfloat16 [1024, 2048], P(('groups', 'ep'), 'rep'), parts along dimension 0
There are 2 independent parts, one for each index of `groups`. A program takes and returns all parts, laid end to end along the dimension named above; an argument that names none is the same for every part. Nothing has to cross between parts.
Inputs may be any that keep to these rules, and one draw needn't show every extreme that they name: `choices`: each row names 8 different experts. In each aligned block of 64 rows no expert is named by more than 64 rows, a bound that some block reaches.
All inputs are finite; a program needn't handle non-finite values.
Results may differ from a plain program's by a relative error of at most 0.0085.
Values may be sent and summed in bfloat16 or wider, within the bound.
A program may use at most 64 MiB of HBM per device.

v0:
```python
import jax
import jax.numpy as jnp
from jax import lax
from jax.sharding import PartitionSpec as P


def local(tokens, choices, route_weight, gate_proj, up_proj, down_proj):
    n_ep = lax.axis_size("ep")
    n_rep = lax.axis_size("rep")
    exp_dev = gate_proj.shape[0]
    num_experts = exp_dev * n_ep
    tok_rows = tokens.shape[0]
    picks = choices.shape[1]
    width = tokens.shape[1]
    slot_cap = min(tok_rows, (2 * tok_rows * picks // num_experts + n_rep - 1) // n_rep * n_rep)
    slot_total = num_experts * slot_cap
    flat_choice = choices.reshape(-1)
    expert_ids = jnp.arange(num_experts, dtype=jnp.int32)
    onehot = (flat_choice[:, None] == expert_ids[None, :]).astype(jnp.int32)
    before = jnp.cumsum(onehot, axis=0) - onehot
    rank = jnp.sum(before * onehot, axis=1)
    slot_ids = flat_choice * slot_cap + rank
    all_slots = jnp.arange(slot_total, dtype=jnp.int32)
    select = (slot_ids[:, None] == all_slots[None, :]).reshape(tok_rows, picks, slot_total)
    dispatch = jnp.sum(select.astype(jnp.bfloat16), axis=1)
    combine = jnp.sum(jnp.where(select, route_weight[:, :, None], 0.0), axis=1)
    combine_high = combine.astype(jnp.bfloat16)
    combine_low = (combine - combine_high.astype(jnp.float32)).astype(jnp.bfloat16)
    buffer = jnp.einsum("ts,td->sd", dispatch, tokens, preferred_element_type=jnp.float32)
    buffer = buffer.astype(jnp.bfloat16).reshape(n_ep, exp_dev, slot_cap, width)
    arrived = lax.all_to_all(buffer, "ep", split_axis=0, concat_axis=0, tiled=True)
    gate_val = jnp.einsum("sjcd,jdh->sjch", arrived, gate_proj, preferred_element_type=jnp.float32)
    up_val = jnp.einsum("sjcd,jdh->sjch", arrived, up_proj, preferred_element_type=jnp.float32)
    hidden = (jax.nn.silu(gate_val) * up_val).astype(jnp.bfloat16)
    partial_out = jnp.einsum(
        "sjch,jhd->sjcd", hidden, down_proj, preferred_element_type=jnp.float32
    )
    expert_out = lax.psum_scatter(
        partial_out.astype(jnp.bfloat16), "rep", scatter_dimension=3, tiled=True
    )
    returned = lax.all_to_all(expert_out, "ep", split_axis=0, concat_axis=0, tiled=True)
    returned_rows = returned.reshape(slot_total, -1)
    mixed = jnp.dot(combine_high, returned_rows, preferred_element_type=jnp.float32)
    mixed = mixed + jnp.dot(combine_low, returned_rows, preferred_element_type=jnp.float32)
    return mixed.astype(jnp.bfloat16)


def solution(mesh):
    placed = (
        P(("groups", "ep"), None),
        P(("groups", "ep"), None),
        P(("groups", "ep"), None),
        P("ep", None, "rep"),
        P("ep", None, "rep"),
        P("ep", "rep", None),
    )
    return jax.shard_map(
        local, mesh=mesh, in_specs=placed, out_specs=P(("groups", "ep"), "rep"), check_vma=False
    )
```

profile of v0, /device:TPU:0, one launch (start us, length us, event | category | flops | bytes accessed | tf_op | source)
XLA Modules:
  0.0 249.3 jit_solution(14430175307891705766)
XLA Ops:
  6.5 0.0 copy-start
  6.5 0.0 reduce-scatter.2.cloned.1.call-start
  6.5 0.9 copy.36
  7.5 0.1 eq.43
  7.6 0.1 eq.39
  7.7 1.2 reduce-window.6
  8.8 0.2 slice_reduce_fusion
  9.1 0.1 fusion.28
  9.2 0.1 reduce_sum.33
  9.3 0.1 copy.39
  9.3 0.7 multiply_add_fusion
  10.0 0.1 copy.40
  10.1 0.7 fusion.21
  10.8 2.2 convolution_convert_fusion
  13.0 0.0 copy-start.3
  13.1 100.4 %all_to_all.10 = bf16[8,2,64,2048]{3,2,1,0:T(8,128)(2,1)S(1)} all-to-all(bf16[8,2,64,2048]{3,2,1,0:T(8,128)(2,1)S(1)} %bitcast.67), channel_id=1, replica_groups=mesh['groups'=2,'ep'=8,'rep'=2] {'ep'}, dimensions={0} | all-to-all | bytes 8388608 | tf_op jit(solution)/shard_map/all_to_all | solution.py:31
  113.5 0.0 copy-start.1
  113.5 2.0 copy-done.1
  115.4 0.0 copy-done.3
  115.4 3.6 %fusion.2 = f32[2,8,64,384]{3,2,1,0:T(8,128)} fusion(bf16[8,2,64,2048]{3,2,1,0:T(8,128)(2,1)S(1)} %all_to_all.10, bf16[2,2048,384]{2,1,0:T(8,128)(2,1)S(1)} %copy-done.3), kind=kOutput, calls=%fused_computation.4 | convolution fusion | flops 1610612736 | bytes 8912896 | tf_op jit(solution)/shard_map/sjcd,jdh->sjch/dot_general | solution.py:32
  119.0 0.0 copy-done
  119.0 8.2 %convert_bitcast_fusion = bf16[8,2,64,2048]{3,2,0,1:T(8,128)(2,1)} fusion(bf16[2,384,2048]{2,1,0:T(8,128)(2,1)S(1)} %copy-done, f32[2,8,64,384]{3,2,1,0:T(8,128)} %fusion.2, bf16[2,2048,384]{2,1,0:T(8,128)(2,1)} %param.10, bf16[8,2,64,2048]{3,2,1,0:T(8,128)(2,1)} %copy-done.1), kind=kOutput, calls=%fused_computation | convolution fusion | flops 3225681920 | bytes 16252928 | tf_op jit(solution)/shard_map/sjch,jhd->sjcd/dot_general | solution.py:35
  127.2 0.0 reduce-scatter.2.cloned.1.call-update
  127.3 53.3 %reduce-scatter.2.cloned.1.call-done = bf16[8,2,64,1024]{3,2,0,1:T(8,128)(2,1)} async-done(((bf16[8,2,64,2048]{3,2,0,1:T(8,128)(2,1)}), bf16[8,2,64,1024]{3,2,0,1:T(8,128)(2,1)}) %reduce-scatter.2.cloned.1.call-update) | async-done | bytes 2097168 | tf_op jit(solution)/shard_map/reduce_scatter | solution.py:38
  180.6 3.2 %copy.44 = bf16[8,2,64,1024]{3,2,1,0:T(8,128)(2,1)} copy(bf16[8,2,64,1024]{3,2,0,1:T(8,128)(2,1)} %reduce-scatter.2.cloned.1.call-done) | data formatting | bytes 4194304 | tf_op jit(solution)/shard_map/reduce_scatter | solution.py:38
  183.8 0.0 copy-start.2
  183.8 4.7 %all-to-all-start.1 = ((bf16[8,2,64,1024]{3,2,1,0:T(8,128)(2,1)}), bf16[8,2,64,1024]{3,2,1,0:T(8,128)(2,1)}, u32[]{:S(2)}, u32[]{:S(2)}) async-start(bf16[8,2,64,1024]{3,2,1,0:T(8,128)(2,1)} %copy.44), calls=%async_computation.2 | async-start | bytes 4194304 | tf_op jit(solution)/shard_map/all_to_all | solution.py:41
  188.5 0.0 copy-done.2
  188.5 0.1 copy.41
  188.6 0.7 select_reduce_fusion
  189.3 48.4 %all-to-all-done.1 = bf16[8,2,64,1024]{3,2,1,0:T(8,128)(2,1)} async-done(((bf16[8,2,64,1024]{3,2,1,0:T(8,128)(2,1)}), bf16[8,2,64,1024]{3,2,1,0:T(8,128)(2,1)}, u32[]{:S(2)}, u32[]{:S(2)}) %all-to-all-start.1) | async-done | bytes 2097184 | tf_op jit(solution)/shard_map/all_to_all | solution.py:41
  237.7 2.1 fusion.24
  239.8 2.7 %fusion.20 = bf16[64,1024]{1,0:T(8,128)(2,1)} fusion(f32[64,1024]{1,0:T(8,128)S(1)} %fusion.24, bf16[1024,1024]{1,0:T(8,128)(2,1)} %bitcast.11, f32[64,1024]{1,0:T(8,128)S(1)} %select_reduce_fusion), kind=kOutput, calls=%fused_computation.20 | convolution fusion | flops 134610944 | bytes 2752512 | tf_op jit(solution)/shard_map/dot_general | solution.py:44
  (3 shorter events, 0.0 us)
Async XLA Ops:
  6.5 112.5 %copy-start = (bf16[2,384,2048]{2,1,0:T(8,128)(2,1)S(1)}, bf16[2,384,2048]{2,1,0:T(8,128)(2,1)}, u32[]{:S(2)}) copy-start(bf16[2,384,2048]{2,1,0:T(8,128)(2,1)} %param.11) | copy-start | bytes 9437188
  6.5 174.1 %reduce-scatter.2.cloned.1.call-start = ((), (), s32[]{:S(2)}) async-start(), calls=%async_computation.3 | async-start | bytes 6291456 | tf_op jit(solution)/shard_map/reduce_scatter | solution.py:38
  13.0 102.4 %copy-start.3 = (bf16[2,2048,384]{2,1,0:T(8,128)(2,1)S(1)}, bf16[2,2048,384]{2,1,0:T(8,128)(2,1)}, u32[]{:S(2)}) copy-start(bf16[2,2048,384]{2,1,0:T(8,128)(2,1)} %param.9) | copy-start | bytes 9437188
  113.5 2.0 copy-start.1
  183.8 4.8 %copy-start.2 = (f32[64,8]{0,1:T(8,128)S(1)}, f32[64,8]{0,1:T(8,128)}, u32[]{:S(2)}) copy-start(f32[64,8]{0,1:T(8,128)} %param.8) | copy-start | bytes 6148
  183.8 53.9 %all-to-all-start.1 = ((bf16[8,2,64,1024]{3,2,1,0:T(8,128)(2,1)}), bf16[8,2,64,1024]{3,2,1,0:T(8,128)(2,1)}, u32[]{:S(2)}, u32[]{:S(2)}) async-start(bf16[8,2,64,1024]{3,2,1,0:T(8,128)(2,1)} %copy.44), calls=%async_computation.2 | async-start | bytes 4194304 | tf_op jit(solution)/shard_map/all_to_all | solution.py:41
Sparse Core Ops, SparseCore 0:
  127.4 53.1 reduce-scatter.1
where the time goes:
time: 250 us; the launch traced here: 249 us
  waiting for transfers between devices  102 us (41%)
  blocking collectives  100 us (40%)
  matrix products  18.8 us (8%)
  between operations  13.5 us (5%)
  local copies, waits for them, and re-layouts  6.8 us (3%)
  starting transfers between devices  4.75 us (2%)
  other arithmetic  3.39 us (1%)
    all_to_all x1, blocking collectives, local(): lax.all_to_all(buffer, 'ep', split_axis=0, concat_axis=0, tiled=True)  100 us
    reduce_scatter x1, waiting for transfers between devices, local(): lax.psum_scatter(partial_out.astype(jnp.bfloat16), 'rep', scatter_dimensi...  53.3 us
    all_to_all x1, waiting for transfers between devices, local(): lax.all_to_all(expert_out, 'ep', split_axis=0, concat_axis=0, tiled=True)  48.4 us
    dot_general x1, matrix products, local(): jnp.einsum('sjch,jhd->sjcd', hidden, down_proj, preferred_element_type=jn...  8.24 us
  transfers between devices with their start and end apart: 2, of which 2 were waited for; matrix products, arithmetic and copies ran while one was open for 0% of the time, Pallas kernels for 0%

commit v1 on v0

--- a/solution.py
+++ b/solution.py
@@ -2,6 +2,31 @@
 import jax.numpy as jnp
 from jax import lax
 from jax.sharding import PartitionSpec as P
+
+
+def tracks_wait(sheet, array_axis, mat):
+    step_out, res = (sheet.shape[:array_axis], sheet.shape[array_axis + 1 :])
+    outcome_arr = sheet.reshape(*step_out, mat, -1, *res)
+    return jnp.moveaxis(outcome_arr, array_axis, 0)
+
+
+def connect_face(frame_in, array_dim):
+    t_next = list(frame_in.shape[1:])
+    t_next[array_dim] *= frame_in.shape[0]
+    return jnp.moveaxis(frame_in, 0, array_dim).reshape(t_next)
+
+
+def stages_all_put(mine_x, original, z, axis_tag):
+    carry_in, front = (lax.axis_size(axis_tag), lax.axis_index(axis_tag))
+    block_next = tracks_wait(z, original, carry_in)
+    rows = [block_next[front]]
+    hop_no = 1
+    while hop_no < carry_in:
+        newest = block_next[front ^ hop_no]
+        rows.append(lax.ppermute(newest, axis_tag, [(it, it ^ hop_no) for it in range(carry_in)]))
+        hop_no += 1
+    block_next = jnp.stack(rows)[front ^ jnp.arange(carry_in)]
+    return connect_face(block_next, mine_x)
 
 
 def local(tokens, choices, route_weight, gate_proj, up_proj, down_proj):
@@ -38,7 +63,7 @@
     expert_out = lax.psum_scatter(
         partial_out.astype(jnp.bfloat16), "rep", scatter_dimension=3, tiled=True
     )
-    returned = lax.all_to_all(expert_out, "ep", split_axis=0, concat_axis=0, tiled=True)
+    returned = stages_all_put(0, 0, expert_out, "ep")
     returned_rows = returned.reshape(slot_total, -1)
     mixed = jnp.dot(combine_high, returned_rows, preferred_element_type=jnp.float32)
     mixed = mixed + jnp.dot(combine_low, returned_rows, preferred_element_type=jnp.float32)

time: 250 us -> 247 us (0.988)
  the two profiles are of different devices: /device:TPU:0 before, /device:TPU:17 now
where the time goes in v1:
time: 247 us
  blocking collectives  95.7 us (39%)
  waiting for transfers between devices  92.7 us (38%)
  matrix products  17.4 us (7%)
  local copies, waits for them, and re-layouts  16.2 us (7%)
  between operations  13.5 us (5%)
  starting transfers between devices  7.72 us (3%)
  other arithmetic  3.41 us (1%)
    all_to_all x1, blocking collectives, local(): lax.all_to_all(buffer, 'ep', split_axis=0, concat_axis=0, tiled=True)  95.7 us
    reduce_scatter x1, waiting for transfers between devices, local(): lax.psum_scatter(partial_out.astype(jnp.bfloat16), 'rep', scatter_dimensi...  55.6 us
    ppermute x7, waiting for transfers between devices, stages_all_put(): lax.ppermute(newest, axis_tag, [(it, it ^ hop_no) for it in range(carry_i...  37 us
    unnamed x19, local copies, waits for them, and re-layouts  9.63 us
    dot_general x1, matrix products, local(): jnp.einsum('sjch,jhd->sjcd', hidden, down_proj, preferred_element_type=jn...  8.24 us
    ppermute x7, starting transfers between devices, stages_all_put(): lax.ppermute(newest, axis_tag, [(it, it ^ hop_no) for it in range(carry_i...  7.72 us
  transfers between devices with their start and end apart: 8, of which 6 were waited for; matrix products, arithmetic and copies ran while one was open for 3% of the time, Pallas kernels for 0%

profile of v1, /device:TPU:17, one launch (start us, length us, event | category | flops | bytes accessed | tf_op | source)
XLA Modules:
  0.0 246.6 jit_solution(8498548859810654235)
XLA Ops:
  6.5 0.0 copy-start
  6.5 0.0 reduce-scatter.2.cloned.1.call-start
  6.5 0.9 copy.57
  7.5 0.1 eq.39
  7.6 0.1 eq.43
  7.7 1.2 reduce-window.6
  8.8 0.2 slice_reduce_fusion
  9.1 0.1 fusion.28
  9.2 0.1 reduce_sum.33
  9.3 0.1 copy.60
  9.3 0.7 multiply_add_fusion
  10.0 0.1 copy.61
  10.1 0.7 fusion.21
  10.8 2.2 convolution_convert_fusion
  13.0 0.0 copy-start.4
  13.0 95.7 %all_to_all.5 = bf16[8,2,64,2048]{3,2,1,0:T(8,128)(2,1)S(1)} all-to-all(bf16[8,2,64,2048]{3,2,1,0:T(8,128)(2,1)S(1)} %bitcast.100), channel_id=1, replica_groups=mesh['groups'=2,'ep'=8,'rep'=2] {'ep'}, dimensions={0} | all-to-all | bytes 8388608 | tf_op jit(solution)/shard_map/all_to_all | solution.py:56
  108.8 0.0 copy-start.2
  108.8 2.0 copy-done.2
  110.8 0.0 copy-done.4
  110.8 3.6 %fusion.2 = f32[2,8,64,384]{3,2,1,0:T(8,128)} fusion(bf16[8,2,64,2048]{3,2,1,0:T(8,128)(2,1)S(1)} %all_to_all.5, bf16[2,2048,384]{2,1,0:T(8,128)(2,1)S(1)} %copy-done.4), kind=kOutput, calls=%fused_computation.5 | convolution fusion | flops 1610612736 | bytes 8912896 | tf_op jit(solution)/shard_map/sjcd,jdh->sjch/dot_general | solution.py:57
  114.3 0.0 copy-done
  114.3 8.2 %convert_bitcast_fusion = bf16[8,2,64,2048]{3,2,0,1:T(8,128)(2,1)} fusion(bf16[2,384,2048]{2,1,0:T(8,128)(2,1)S(1)} %copy-done, f32[2,8,64,384]{3,2,1,0:T(8,128)} %fusion.2, bf16[2,2048,384]{2,1,0:T(8,128)(2,1)} %param.10, bf16[8,2,64,2048]{3,2,1,0:T(8,128)(2,1)} %copy-done.2), kind=kOutput, calls=%fused_computation.1 | convolution fusion | flops 3225681920 | bytes 16252928 | tf_op jit(solution)/shard_map/sjch,jhd->sjcd/dot_general | solution.py:60
  122.6 0.0 copy-start.3
  122.6 0.0 reduce-scatter.2.cloned.1.call-update
  122.6 0.6 copy-done.3
  123.2 0.1 copy.62
  123.3 55.6 %reduce-scatter.2.cloned.1.call-done = bf16[8,2,64,1024]{3,2,0,1:T(8,128)(2,1)} async-done(((bf16[8,2,64,2048]{3,2,0,1:T(8,128)(2,1)}), bf16[8,2,64,1024]{3,2,0,1:T(8,128)(2,1)}) %reduce-scatter.2.cloned.1.call-update) | async-done | bytes 2097168 | tf_op jit(solution)/shard_map/reduce_scatter | solution.py:63
  179.0 1.6 constant_dynamic-slice_fusion
  180.6 0.7 collective-permute-start
  181.3 0.7 select_reduce_fusion
  182.1 1.3 collective-permute-start.1
  183.3 0.4 collective-permute-start.2
  183.8 0.2 collective-permute-start.3
  184.0 2.5 %collective-permute-start.4 = (bf16[1,2,64,1024]{3,2,1,0:T(8,128)(2,1)S(1)}, bf16[1,2,64,1024]{3,2,1,0:T(8,128)(2,1)S(1)}, u32[]{:S(2)}, u32[]{:S(2)}) collective-permute-start(bf16[1,2,64,1024]{3,2,1,0:T(8,128)(2,1)S(1)} %get-tuple-element.6), channel_id=1, source_target_pairs={{0,10},{2,8},{4,14},{6,12},{8,2},{10,0},{12,6},{14,4},{1,11},{3,9}... | collective-permute-start | bytes 786440 | tf_op jit(solution)/shard_map/ppermute | solution.py:26
  186.5 1.7 bitcast_dynamic-update-slice_fusion.7
  188.2 0.0 collective-permute-done
  188.2 0.3 collective-permute-start.5
  188.5 0.7 bitcast_dynamic-update-slice_fusion.6
  189.2 8.6 %collective-permute-done.1 = bf16[1,2,64,1024]{3,2,1,0:T(8,128)(2,1)S(1)} collective-permute-done((bf16[1,2,64,1024]{3,2,1,0:T(8,128)(2,1)S(1)}, bf16[1,2,64,1024]{3,2,1,0:T(8,128)(2,1)S(1)}, u32[]{:S(2)}, u32[]{:S(2)}) %collective-permute-start.1) | collective-permute-done | bytes 262176 | tf_op jit(solution)/shard_map/ppermute | solution.py:26
  197.8 2.3 collective-permute-start.6
  200.0 0.7 bitcast_dynamic-update-slice_fusion.5
  200.8 2.6 %collective-permute-done.2 = bf16[1,2,64,1024]{3,2,1,0:T(8,128)(2,1)S(1)} collective-permute-done((bf16[1,2,64,1024]{3,2,1,0:T(8,128)(2,1)S(1)}, bf16[1,2,64,1024]{3,2,1,0:T(8,128)(2,1)S(1)}, u32[]{:S(2)}, u32[]{:S(2)}) %collective-permute-start.2) | collective-permute-done | bytes 262176 | tf_op jit(solution)/shard_map/ppermute | solution.py:26
  203.4 0.7 bitcast_dynamic-update-slice_fusion.4
  204.1 0.0 collective-permute-done.3
  204.1 0.7 bitcast_dynamic-update-slice_fusion.3
  204.9 2.6 %collective-permute-done.4 = bf16[1,2,64,1024]{3,2,1,0:T(8,128)(2,1)S(1)} collective-permute-done((bf16[1,2,64,1024]{3,2,1,0:T(8,128)(2,1)S(1)}, bf16[1,2,64,1024]{3,2,1,0:T(8,128)(2,1)S(1)}, u32[]{:S(2)}, u32[]{:S(2)}) %collective-permute-start.4) | collective-permute-done | bytes 262176 | tf_op jit(solution)/shard_map/ppermute | solution.py:26
  207.5 0.7 bitcast_dynamic-update-slice_fusion.2
  208.2 17.9 %collective-permute-done.5 = bf16[1,2,64,1024]{3,2,1,0:T(8,128)(2,1)S(1)} collective-permute-done((bf16[1,2,64,1024]{3,2,1,0:T(8,128)(2,1)S(1)}, bf16[1,2,64,1024]{3,2,1,0:T(8,128)(2,1)S(1)}, u32[]{:S(2)}, u32[]{:S(2)}) %collective-permute-start.5) | collective-permute-done | bytes 262176 | tf_op jit(solution)/shard_map/ppermute | solution.py:26
  226.2 0.7 bitcast_dynamic-update-slice_fusion.1
  226.9 5.2 %collective-permute-done.6 = bf16[1,2,64,1024]{3,2,0,1:T(8,128)(2,1)S(1)} collective-permute-done((bf16[1,2,64,1024]{3,2,0,1:T(8,128)(2,1)S(1)}, bf16[1,2,64,1024]{3,2,0,1:T(8,128)(2,1)S(1)}, u32[]{:S(2)}, u32[]{:S(2)}) %collective-permute-start.6) | collective-permute-done | bytes 262176 | tf_op jit(solution)/shard_map/ppermute | solution.py:26
  232.1 0.7 bitcast_dynamic-update-slice_fusion
  232.8 3.6 %gather_fusion = bf16[8,2,64,1024]{3,2,1,0:T(8,128)(2,1)} fusion(bf16[8,2,64,1024]{3,2,1,0:T(8,128)(2,1)} %bitcast.19, s32[1024]{0:T(1024)S(1)} %pad_clamp_fusion), kind=kCustom, calls=%fused_computation | custom fusion | bytes 4194336 | tf_op jit(solution)/shard_map/gather | solution.py:28
  236.4 0.0 copy-start.1
  236.4 2.2 fusion.24
  238.6 0.0 copy-done.1
  238.6 1.1 fusion.20
  (5 shorter events, 0.1 us)
Async XLA Ops:
  6.5 107.8 %copy-start = (bf16[2,384,2048]{2,1,0:T(8,128)(2,1)S(1)}, bf16[2,384,2048]{2,1,0:T(8,128)(2,1)}, u32[]{:S(2)}) copy-start(bf16[2,384,2048]{2,1,0:T(8,128)(2,1)} %param.11) | copy-start | bytes 9437188
  6.5 172.5 %reduce-scatter.2.cloned.1.call-start = ((), (), s32[]{:S(2)}) async-start(), calls=%async_computation.2 | async-start | bytes 6291456 | tf_op jit(solution)/shard_map/reduce_scatter | solution.py:63
  13.0 97.7 %copy-start.4 = (bf16[2,2048,384]{2,1,0:T(8,128)(2,1)S(1)}, bf16[2,2048,384]{2,1,0:T(8,128)(2,1)}, u32[]{:S(2)}) copy-start(bf16[2,2048,384]{2,1,0:T(8,128)(2,1)} %param.9) | copy-start | bytes 9437188
  108.8 2.0 copy-start.2
  122.6 0.7 copy-start.3
  180.6 7.6 %collective-permute-start = (bf16[1,2,64,1024]{3,2,1,0:T(8,128)(2,1)S(1)}, bf16[1,2,64,1024]{3,2,1,0:T(8,128)(2,1)S(1)}, u32[]{:S(2)}, u32[]{:S(2)}) collective-permute-start(bf16[1,2,64,1024]{3,2,1,0:T(8,128)(2,1)S(1)} %get-tuple-element.10), channel_id=1, source_target_pairs={{0,2},{2,0},{4,6},{6,4},{8,10},{10,8},{12,14},{14,12},{1,3},{3,1},... | collective-permute-start | bytes 786440 | tf_op jit(solution)/shard_map/ppermute | solution.py:26
  182.1 15.7 %collective-permute-start.1 = (bf16[1,2,64,1024]{3,2,1,0:T(8,128)(2,1)S(1)}, bf16[1,2,64,1024]{3,2,1,0:T(8,128)(2,1)S(1)}, u32[]{:S(2)}, u32[]{:S(2)}) collective-permute-start(bf16[1,2,64,1024]{3,2,1,0:T(8,128)(2,1)S(1)} %get-tuple-element.9), channel_id=1, source_target_pairs={{0,4},{2,6},{4,0},{6,2},{8,12},{10,14},{12,8},{14,10},{1,5},{3,7},... | collective-permute-start | bytes 786440 | tf_op jit(solution)/shard_map/ppermute | solution.py:26
  183.3 20.1 %collective-permute-start.2 = (bf16[1,2,64,1024]{3,2,1,0:T(8,128)(2,1)S(1)}, bf16[1,2,64,1024]{3,2,1,0:T(8,128)(2,1)S(1)}, u32[]{:S(2)}, u32[]{:S(2)}) collective-permute-start(bf16[1,2,64,1024]{3,2,1,0:T(8,128)(2,1)S(1)} %get-tuple-element.8), channel_id=1, source_target_pairs={{0,6},{2,4},{4,2},{6,0},{8,14},{10,12},{12,10},{14,8},{1,7},{3,5},... | collective-permute-start | bytes 786440 | tf_op jit(solution)/shard_map/ppermute | solution.py:26
  183.8 20.3 %collective-permute-start.3 = (bf16[1,2,64,1024]{3,2,1,0:T(8,128)(2,1)S(1)}, bf16[1,2,64,1024]{3,2,1,0:T(8,128)(2,1)S(1)}, u32[]{:S(2)}, u32[]{:S(2)}) collective-permute-start(bf16[1,2,64,1024]{3,2,1,0:T(8,128)(2,1)S(1)} %get-tuple-element.7), channel_id=1, source_target_pairs={{0,8},{2,10},{4,12},{6,14},{8,0},{10,2},{12,4},{14,6},{1,9},{3,11}... | collective-permute-start | bytes 786440 | tf_op jit(solution)/shard_map/ppermute | solution.py:26
  184.0 23.5 %collective-permute-start.4 = (bf16[1,2,64,1024]{3,2,1,0:T(8,128)(2,1)S(1)}, bf16[1,2,64,1024]{3,2,1,0:T(8,128)(2,1)S(1)}, u32[]{:S(2)}, u32[]{:S(2)}) collective-permute-start(bf16[1,2,64,1024]{3,2,1,0:T(8,128)(2,1)S(1)} %get-tuple-element.6), channel_id=1, source_target_pairs={{0,10},{2,8},{4,14},{6,12},{8,2},{10,0},{12,6},{14,4},{1,11},{3,9}... | collective-permute-start | bytes 786440 | tf_op jit(solution)/shard_map/ppermute | solution.py:26
  188.2 38.0 %collective-permute-start.5 = (bf16[1,2,64,1024]{3,2,1,0:T(8,128)(2,1)S(1)}, bf16[1,2,64,1024]{3,2,1,0:T(8,128)(2,1)S(1)}, u32[]{:S(2)}, u32[]{:S(2)}) collective-permute-start(bf16[1,2,64,1024]{3,2,1,0:T(8,128)(2,1)S(1)} %get-tuple-element.11), channel_id=1, source_target_pairs={{0,12},{2,14},{4,8},{6,10},{8,4},{10,6},{12,0},{14,2},{1,13},{3,15... | collective-permute-start | bytes 786440 | tf_op jit(solution)/shard_map/ppermute | solution.py:26
  197.8 34.3 %collective-permute-start.6 = (bf16[1,2,64,1024]{3,2,0,1:T(8,128)(2,1)S(1)}, bf16[1,2,64,1024]{3,2,0,1:T(8,128)(2,1)S(1)}, u32[]{:S(2)}, u32[]{:S(2)}) collective-permute-start(bf16[1,2,64,1024]{3,2,0,1:T(8,128)(2,1)S(1)} %get-tuple-element.5), channel_id=1, source_target_pairs={{0,14},{2,12},{4,10},{6,8},{8,6},{10,4},{12,2},{14,0},{1,15},{3,13... | collective-permute-start | bytes 786440 | tf_op jit(solution)/shard_map/ppermute | solution.py:26
  236.4 2.2 copy-start.1
Sparse Core Ops, SparseCore 0:
  122.7 56.2 reduce-scatter.1
